TPU v7x, 256 devices: a whole 4x4x8 slice. The times are simulated.
256 devices in a mesh: row: 64 (over y, z, core), col: 4 (over x).
Axes of the slice: x: 4, y: 4, z: 8, core: 2. Of those that a mesh axis runs over, the one named last changes fastest.
Arguments:
- entity_feats: bfloat16 [65536, 256], P(('col', 'row')), may hold values from -6 to 6
- class_map: int32 [65536], P(('col', 'row')), may hold values from 0 to 127, as said below
- tile_values: bfloat16 [8192, 128, 128], P(('row', 'col')), may hold values from -0.09375 to 0.09375
- tile_rows: int32 [8192], P(('row', 'col')), may hold values from 0 to 3
- tile_column_index: int32 [8192], P(('row', 'col')), may hold values from 0 to 63
- tile_rels: int32 [8192], P(('row', 'col')), may hold values from 0 to 499
- tile_counts: int32 [256], P(('row', 'col')), may hold values from 4 to 32, as said below
- coefficients: bfloat16 [500, 8], replicated, may hold values from -2 to 2
- bases: bfloat16 [8, 256, 256], replicated, may hold values from -0.375 to 0.375
- cotangent: bfloat16 [32768, 256], P(('row', 'col')), may hold values from -6 to 6
Outputs:
- layer_out: bfloat16 [32768, 256], P(('row', 'col'))
- grad_entities: float32 [65536, 256], P(('col', 'row'))
- grad_bases: float32 [8, 256, 256], replicated
- grad_coef: float32 [500, 8], replicated
Inputs may be any that keep to these rules, and one draw needn't show every extreme that they name: `class_map`: within every block of 256 entities, every class number 0 to 127 occurs at least once. `tile_counts`: tile slots of a device from its count onward are unused; some device has all 32 slots live in every draw.
All inputs are finite; a program needn't handle non-finite values.
Results may differ from a plain program's by a relative error of at most 0.006.
Values may be sent and summed in bfloat16 or wider, within the bound.
No kernel may reach another device: no remote copies, remote signals or barrier semaphores. Data moves between devices by JAX's collectives and lax.ppermute only.
A program may use at most 128 MiB of HBM per device.

v0:
```python
import jax
import jax.numpy as jnp
from jax import lax
from jax.sharding import PartitionSpec as P

TBLK = 32


def tile_weights(rel_block, row_block, live, coefficients, trows, relations):
    pick_rel = (rel_block[:, None] == jnp.arange(relations, dtype=jnp.int32)[None, :]).astype(
        jnp.bfloat16
    )
    coef_rows = jnp.dot(pick_rel, coefficients, preferred_element_type=jnp.float32)
    pick_row = (
        (row_block[:, None] == jnp.arange(trows, dtype=jnp.int32)[None, :]) & live[:, None]
    ).astype(jnp.float32)
    weights = (pick_row[:, :, None] * coef_rows[:, None, :]).astype(jnp.bfloat16)
    return (weights, pick_row)


def local(
    entity_feats,
    class_map,
    tile_values,
    tile_rows,
    tile_column_index,
    tile_rels,
    tile_counts,
    coefficients,
    bases,
    cotangent,
):
    n_row = lax.axis_size("row")
    n_col = lax.axis_size("col")
    node_dev = cotangent.shape[0]
    tile = tile_values.shape[1]
    nbases = bases.shape[0]
    width = bases.shape[1]
    relations = coefficients.shape[0]
    rblock = node_dev * n_col
    cblock = node_dev * n_row
    trows = rblock // tile
    tile_column_list = cblock // tile
    member = class_map[:, None] == jnp.arange(node_dev, dtype=jnp.int32)[None, :]
    member_bf = member.astype(jnp.bfloat16)
    sums = lax.dot_general(
        member_bf, entity_feats, (((0,), (0,)), ((), ())), preferred_element_type=jnp.float32
    )
    counts = jnp.sum(member.astype(jnp.float32), axis=0)
    class_feat = (sums / counts[:, None]).astype(jnp.bfloat16)
    sender_device = lax.all_gather(class_feat, "row", axis=0, tiled=True).reshape(
        tile_column_list, tile, width
    )
    stacked = bases.reshape(nbases * width, width)
    live_count = tile_counts[0]
    turns = (live_count + TBLK - 1) // TBLK

    def forward_turn(step, carry):
        sums_acc, msg_store = carry
        leading_entry = step * TBLK
        live = leading_entry + jnp.arange(TBLK, dtype=jnp.int32) < live_count
        selected_entries = jnp.take(sender_device, tile_column_index, axis=0)
        messages = jnp.einsum(
            "kij,kjh->kih", tile_values, selected_entries, preferred_element_type=jnp.float32
        ).astype(jnp.bfloat16)
        weights, pick_row = tile_weights(tile_rels, tile_rows, live, coefficients, trows, relations)
        sums_acc = sums_acc + jnp.einsum(
            "ktb,kih->tibh", weights, messages, preferred_element_type=jnp.float32
        )
        msg_store = messages
        return (sums_acc, msg_store)

    init_sums = jnp.zeros((trows, tile, nbases, width), jnp.float32)
    init_store = jnp.zeros((tile_values.shape[0], tile, width), jnp.bfloat16)
    sums_acc, msg_store = lax.fori_loop(0, turns, forward_turn, (init_sums, init_store))
    part = sums_acc.astype(jnp.bfloat16).reshape(rblock, nbases * width)
    out_part = jnp.dot(part, stacked, preferred_element_type=jnp.float32)
    layer_out = lax.psum_scatter(out_part, "col", scatter_dimension=0, tiled=True).astype(
        jnp.bfloat16
    )
    dout_rows = lax.all_gather(cotangent, "col", axis=0, tiled=True)
    grads_rows = lax.dot_general(
        dout_rows, stacked, (((1,), (1,)), ((), ())), preferred_element_type=jnp.float32
    ).astype(jnp.bfloat16)
    dv_part = lax.dot_general(
        part, dout_rows, (((0,), (0,)), ((), ())), preferred_element_type=jnp.float32
    )
    grads_tiles = grads_rows.reshape(trows, tile, nbases, width)

    def backward_turn(step, carry):
        dcoef_acc, dx_acc = carry
        leading_entry = step * TBLK
        live = leading_entry + jnp.arange(TBLK, dtype=jnp.int32) < live_count
        weights, pick_row = tile_weights(tile_rels, tile_rows, live, coefficients, trows, relations)
        gram = jnp.einsum(
            "kih,tibh->ktb", msg_store, grads_tiles, preferred_element_type=jnp.float32
        )
        per_tile = jnp.sum(gram * pick_row[:, :, None], axis=1)
        dcoef_acc = dcoef_acc + jax.ops.segment_sum(per_tile, tile_rels, num_segments=relations)
        mixed = jnp.einsum(
            "ktb,tibh->kih", weights, grads_tiles, preferred_element_type=jnp.float32
        ).astype(jnp.bfloat16)
        back = jnp.einsum("kij,kih->kjh", tile_values, mixed, preferred_element_type=jnp.float32)
        dx_acc = dx_acc.at[tile_column_index].add(back)
        return (dcoef_acc, dx_acc)

    init_coef = jnp.zeros((relations, nbases), jnp.float32)
    init_dx = jnp.zeros((tile_column_list, tile, width), jnp.float32)
    dcoef_acc, dx_acc = lax.fori_loop(0, turns, backward_turn, (init_coef, init_dx))
    dx_all = dx_acc.reshape(cblock, width)
    dx_own = lax.psum_scatter(dx_all, "row", scatter_dimension=0, tiled=True)
    dv_sum, dcoef_sum = lax.psum((dv_part, dcoef_acc), ("row", "col"))
    scale = (node_dev * n_row * n_col) ** (-0.5)
    grad_bases = (dv_sum * scale).reshape(nbases, width, width)
    grad_coef = dcoef_sum * scale
    quotient = dx_own / counts[:, None]
    grad_entities = jnp.dot(member.astype(jnp.float32), quotient, precision=lax.Precision.HIGHEST)
    return (layer_out, grad_entities, grad_bases, grad_coef)


def solution(mesh):
    placed = (
        P(("col", "row"), None),
        P(("col", "row")),
        P(("row", "col"), None, None),
        P(("row", "col")),
        P(("row", "col")),
        P(("row", "col")),
        P(("row", "col")),
        P(),
        P(),
        P(("row", "col"), None),
    )
    return jax.shard_map(
        local,
        mesh=mesh,
        in_specs=placed,
        out_specs=(P(("row", "col"), None), P(("col", "row"), None), P(), P()),
        check_vma=False,
    )
```

profile of v0, /device:TPU:2, one launch (start us, length us, event | category | flops | bytes accessed | tf_op | source)
XLA Modules:
  0.0 570.0 jit_solution(12668102719578885372)
XLA Ops:
  7.2 0.9 convert_reduce_fusion
  8.1 1.8 fusion.22
  10.7 12.6 %all_gather.7 = bf16[512,256]{1,0:T(8,128)(2,1)S(1)} all-gather(bf16[128,256]{1,0:T(8,128)(2,1)} %param.23), channel_id=1, replica_groups=mesh['row'=64,'col'=4] {'col'}, dimensions={0}, use_global_device_ids=true | all-gather | bytes 327680 | tf_op jit(solution)/shard_map/all_gather | solution.py:81
  23.3 0.7 compare_select_fusion.1
  23.9 0.7 compare_and_fusion
  24.6 0.9 fusion.32
  25.5 67.9 %all-gather.2.cloned.1.call-done = bf16[8192,256]{1,0:T(8,128)(2,1)} async-done(((bf16[128,256]{1,0:T(8,128)(2,1)}), bf16[8192,256]{1,0:T(8,128)(2,1)}) %all-gather.2.cloned.1.call-update) | async-done | bytes 4194320 | tf_op jit(solution)/shard_map/all_gather | solution.py:51
  93.4 4.3 gather_fusion
  97.7 3.8 convert_bitcast_fusion
  101.4 3.4 copy.35
  104.8 1.6 broadcast_in_dim.33
  106.4 2.3 broadcast_in_dim.32
  108.7 6.6 %while.31 = (s32[]{:T(128)}, f32[4,128,8,256]{3,2,1,0:T(8,128)}, bf16[32,128,256]{2,0,1:T(8,128)(2,1)}, s32[]{:T(128)}, s32[32]{0:T(128)S(1)}, /*index=5*/s32[]{...) while((s32[]{:T(128)}, f32[4,128,8,256]{3,2,1,0:T(8,128)}, ...), condition=%wide.region_2.3_spmd, body=%wide.region_1.2_spmd.sunk | while | flops 68159936 | bytes 48236912 | solution.py:75
  108.7 0.7 add_compare_fusion.4
  109.4 1.3 copy.62
  110.7 1.6 copy-done.1
  112.3 1.1 bitcast_add_fusion.2
  113.4 1.9 copy-done.2
  115.3 2.4 convert_element_type.73
  117.7 0.7 copy.42
  118.4 1.3 copy-done.5
  119.8 2.1 fusion.37
  121.9 0.7 convolution_convert_fusion
  122.7 0.7 copy.43
  123.4 0.3 copy.36
  123.6 1.3 copy-done.7
  124.9 0.7 fusion.23
  125.6 0.9 copy-done.6
  126.5 1.5 fusion.36
  128.2 4.3 broadcast_in_dim.46
  132.4 22.2 %while.32 = (s32[]{:T(128)}, f32[500,8]{1,0:T(8,128)S(1)}, f32[64,128,256]{2,1,0:T(8,128)}, s32[]{:T(128)}, s32[32]{0:T(128)S(1)}, /*index=5*/s32[32]{0:T(128)S(...) while((s32[]{:T(128)}, f32[500,8]{1,0:T(8,128)S(1)}, ...), condition=%wide.region_8.9_spmd, body=%wide.region_4.8_spmd.sunk | while | flops 337646112 | bytes 36713844 | solution.py:109
  132.4 0.7 add_compare_fusion.5
  133.1 0.1 copy.50
  133.2 0.8 scatter_fusion
  134.1 0.7 bitcast_convert_fusion.2
  134.8 0.5 copy-done.4
  135.3 3.7 convolution_bitcast_fusion.2
  139.0 5.6 copy.51
  144.6 10.1 %scatter_fusion.1 = f32[64,128,256]{2,1,0:T(8,128)} fusion(f32[64,128,256]{2,1,0:T(8,128)} %get-tuple-element.645, s32[32]{0:T(128)S(1)} %fusion.66, f32[32,128,256]{2,1,0:T(8,128)} %copy.51), kind=kCustom, calls=%fused_computation.2.clone.1 | custom fusion | flops 1048576 | bytes 12583040 | tf_op jit(solution)/shard_map/while/body/scatter-add | solution.py:104
  154.7 0.1 copy.37
  154.8 75.1 %psum.15 = f32[500,8]{0,1:T(8,128)S(1)} all-reduce(f32[500,8]{0,1:T(8,128)S(1)} %copy.37), channel_id=1, replica_groups=mesh['row'=64,'col'=4] {'row','col'}, use_global_device_ids=true, to_apply=%region_11.12 | all-reduce | flops 4000 | bytes 32000 | tf_op jit(solution)/shard_map/psum | solution.py:112
  229.9 0.6 broadcast_multiply_fusion.1
  230.5 150.1 %all-reduce.2.cloned.1.call-done = f32[2048,256]{1,0:T(8,128)} async-done(((f32[2048,256]{1,0:T(8,128)}), f32[2048,256]{1,0:T(8,128)}) %all-reduce.2.cloned.1.call-update) | async-done | bytes 2097168 | tf_op jit(solution)/shard_map/psum | solution.py:112
  380.6 3.1 broadcast_multiply_fusion
  383.7 20.1 %reduce-scatter.3.cloned.1.call-done = f32[128,256]{1,0:T(8,128)} async-done(((f32[512,256]{1,0:T(8,128)}), f32[128,256]{1,0:T(8,128)}) %reduce-scatter.3.cloned.1.call-update) | async-done | bytes 131088 | tf_op jit(solution)/shard_map/reduce_scatter | solution.py:78
  403.8 1.5 convert_element_type.74
  405.3 156.1 %reduce-scatter.5.cloned.1.call-done = f32[128,256]{1,0:T(8,128)} async-done(((f32[8192,256]{1,0:T(8,128)}), f32[128,256]{1,0:T(8,128)}) %reduce-scatter.5.cloned.1.call-update) | async-done | bytes 131088 | tf_op jit(solution)/shard_map/reduce_scatter | solution.py:111
  561.5 2.0 fusion.27
  (32 shorter events, 0.3 us)
Async XLA Ops:
  7.2 114.7 %copy-start = (bf16[8,256,256]{2,1,0:T(8,128)(2,1)S(1)}, bf16[8,256,256]{2,1,0:T(8,128)(2,1)}, u32[]{:S(2)}) copy-start(bf16[8,256,256]{2,1,0:T(8,128)(2,1)} %param.22) | copy-start | bytes 3145732
  7.2 86.2 %all-gather.2.cloned.1.call-start = ((), (), s32[]{:S(2)}) async-start(), calls=%async_computation.2 | async-start | bytes 4259840 | tf_op jit(solution)/shard_map/all_gather | solution.py:51
  10.0 370.7 %all-reduce.2.cloned.1.call-start = ((), (), s32[]{:S(2)}) async-start(), calls=%async_computation.5 | async-start | bytes 4194304 | tf_op jit(solution)/shard_map/psum | solution.py:112
  93.4 4.3 copy-start.3
  106.4 2.3 copy-start.8
  109.4 2.9 copy-start.1
  113.4 1.9 copy-start.2
  118.4 1.3 copy-start.5
  121.9 282.0 %reduce-scatter.3.cloned.1.call-start = ((), (), s32[]{:S(2)}) async-start(), calls=%async_computation.3 | async-start | bytes 655360 | tf_op jit(solution)/shard_map/reduce_scatter | solution.py:78
  123.3 1.6 copy-start.7
  124.9 1.6 copy-start.6
  128.1 433.4 %reduce-scatter.5.cloned.1.call-start = ((), (), s32[]{:S(2)}) async-start(), calls=%async_computation.4 | async-start | bytes 8519680 | tf_op jit(solution)/shard_map/reduce_scatter | solution.py:111
  128.2 4.3 copy-start.9
  128.2 4.3 copy-start.11
  134.1 1.2 copy-start.4
  230.5 331.0 %copy-start.10 = (s32[256]{0:T(256)S(1)}, s32[256]{0:T(256)}, u32[]{:S(2)}) copy-start(s32[256]{0:T(256)} %param.15) | copy-start | bytes 3076
Sparse Core Ops, SparseCore 0:
  11.4 81.9 all-gather.1
  122.0 258.6 all-reduce.1
  383.2 20.6 reduce-scatter.2
  407.9 153.5 reduce-scatter.4
where the time goes:
time: 571 us; the launch traced here: 570 us
  waiting for transfers between devices  394 us (69%)
  blocking collectives  87.6 us (15%)
  local copies, waits for them, and re-layouts  32.2 us (6%)
  other arithmetic  22.1 us (4%)
  matrix products  18.9 us (3%)
  between operations  14.5 us (3%)
    reduce_scatter x1, waiting for transfers between devices, local(): dx_own = lax.psum_scatter(dx_all, 'row', scatter_dimension=0, tiled=True)  156 us
    psum x1, waiting for transfers between devices, local(): dv_sum, dcoef_sum = lax.psum((dv_part, dcoef_acc), ('row', 'col'))  150 us
    psum x1, blocking collectives, local(): dv_sum, dcoef_sum = lax.psum((dv_part, dcoef_acc), ('row', 'col'))  75.1 us
    all_gather x1, waiting for transfers between devices, local(): lax.all_gather(class_feat, 'row', axis=0, tiled=True)  67.9 us
    reduce_scatter x1, waiting for transfers between devices, local(): lax.psum_scatter(out_part, 'col', scatter_dimension=0, tiled=True)  20.1 us
    all_gather x1, blocking collectives, local(): dout_rows = lax.all_gather(cotangent, 'col', axis=0, tiled=True)  12.6 us
  transfers between devices with their start and end apart: 4, of which 4 were waited for; matrix products, arithmetic and copies ran while one was open for 7% of the time, Pallas kernels for 0%

commit v1 on v0

--- a/solution.py
+++ b/solution.py
@@ -1,9 +1,25 @@
+import functools
 import jax
 import jax.numpy as jnp
 from jax import lax
 from jax.sharding import PartitionSpec as P
 
 TBLK = 32
+
+
+def _process_indices(incoming_x, ax_name):
+    return jnp.concatenate(
+        jax.lax.all_to_all(
+            jnp.stack([incoming_x] * jax.lax.psum(1, axis_name=ax_name), 0),
+            concat_axis=0,
+            axis_name=ax_name,
+            split_axis=0,
+        ),
+        0,
+    )
+
+
+page_convert = functools.partial(_process_indices, ax_name="row")
 
 
 def tile_weights(rel_block, row_block, live, coefficients, trows, relations):
@@ -48,9 +64,7 @@
     )
     counts = jnp.sum(member.astype(jnp.float32), axis=0)
     class_feat = (sums / counts[:, None]).astype(jnp.bfloat16)
-    sender_device = lax.all_gather(class_feat, "row", axis=0, tiled=True).reshape(
-        tile_column_list, tile, width
-    )
+    sender_device = page_convert(class_feat).reshape(tile_column_list, tile, width)
     stacked = bases.reshape(nbases * width, width)
     live_count = tile_counts[0]
     turns = (live_count + TBLK - 1) // TBLK

time: 571 us -> 426 us (0.75)
  waiting for transfers between devices: 394 us -> 236 us
  starting transfers between devices: 0.16 us -> 12.6 us
    reduce_scatter x1, waiting for transfers between devices: 156 us -> 0.01 us  [local(): dx_own = lax.psum_scatter(dx_all, 'row', scatter_dimension=0, tiled=True)]
    all_to_all x0 -> x1, waiting for transfers between devices: none -> 82.4 us  [_process_indices(): jax.lax.all_to_all(jnp.stack([incoming_x] * jax.lax.psum(1, axis_name=ax_...]
    all_gather x1 -> x0, waiting for transfers between devices: 67.9 us -> none  [local(): lax.all_gather(class_feat, 'row', axis=0, tiled=True)]
    reduce_scatter x1, waiting for transfers between devices: 20.1 us -> 0.01 us  [local(): lax.psum_scatter(out_part, 'col', scatter_dimension=0, tiled=True)]
    all_to_all x0 -> x1, starting transfers between devices: none -> 12.5 us  [_process_indices(): jax.lax.all_to_all(jnp.stack([incoming_x] * jax.lax.psum(1, axis_name=ax_...]
  transfers between devices with their start and end apart: 4 -> 4, of which waited for: 4 -> 2; matrix products, arithmetic and copies ran while one was open for 7% -> 8% of each run, Pallas kernels for 0% -> 0%
where the time goes in v1:
time: 426 us; the launch traced here: 425 us
  waiting for transfers between devices  236 us (55%)
  blocking collectives  86.7 us (20%)
  local copies, waits for them, and re-layouts  34.6 us (8%)
  other arithmetic  20.9 us (5%)
  matrix products  17.6 us (4%)
  between operations  16.3 us (4%)
  starting transfers between devices  12.6 us (3%)
    psum x1, waiting for transfers between devices, local(): dv_sum, dcoef_sum = lax.psum((dv_part, dcoef_acc), ('row', 'col'))  154 us
    all_to_all x1, waiting for transfers between devices, _process_indices(): jax.lax.all_to_all(jnp.stack([incoming_x] * jax.lax.psum(1, axis_name=ax_...  82.4 us
    psum x1, blocking collectives, local(): dv_sum, dcoef_sum = lax.psum((dv_part, dcoef_acc), ('row', 'col'))  74.4 us
    all_to_all x1, starting transfers between devices, _process_indices(): jax.lax.all_to_all(jnp.stack([incoming_x] * jax.lax.psum(1, axis_name=ax_...  12.5 us
    all_gather x1, blocking collectives, local(): dout_rows = lax.all_gather(cotangent, 'col', axis=0, tiled=True)  12.3 us
    scatter-add x1, other arithmetic, backward_turn(): dx_acc = dx_acc.at[tile_column_index].add(back)  10.2 us
  transfers between devices with their start and end apart: 4, of which 2 were waited for; matrix products, arithmetic and copies ran while one was open for 8% of the time, Pallas kernels for 0%

profile of v1, /device:TPU:2, one launch (start us, length us, event | category | flops | bytes accessed | tf_op | source)
XLA Modules:
  0.0 425.3 jit_solution(12187946912423753669)
XLA Ops:
  8.0 0.9 convert_reduce_fusion
  8.9 1.2 fusion.22
  10.1 2.5 stack.2
  12.6 12.5 %all-to-all-start = ((bf16[64,128,256]{2,1,0:T(8,128)(2,1)}), bf16[64,128,256]{2,1,0:T(8,128)(2,1)}, u32[]{:S(2)}, u32[]{:S(2)}) async-start(bf16[64,128,256]{2,1,0:T(8,128)(2,1)} %stack.2), calls=%async_computation | async-start | bytes 8388608 | tf_op jit(solution)/shard_map/all_to_all | solution.py:12
  25.8 12.3 %all_gather.3 = bf16[512,256]{1,0:T(8,128)(2,1)S(1)} all-gather(bf16[128,256]{1,0:T(8,128)(2,1)S(1)} %copy-done.8), channel_id=1, replica_groups=mesh['row'=64,'col'=4] {'col'}, dimensions={0}, use_global_device_ids=true | all-gather | bytes 327680 | tf_op jit(solution)/shard_map/all_gather | solution.py:95
  38.2 0.2 fusion.32
  38.4 82.4 %all-to-all-done = bf16[64,128,256]{2,1,0:T(8,128)(2,1)} async-done(((bf16[64,128,256]{2,1,0:T(8,128)(2,1)}), bf16[64,128,256]{2,1,0:T(8,128)(2,1)}, u32[]{:S(2)}, u32[]{:S(2)}) %all-to-all-start) | async-done | bytes 4194336 | tf_op jit(solution)/shard_map/all_to_all | solution.py:12
  120.8 4.2 gather_fusion
  125.0 3.8 convert_bitcast_fusion
  128.8 3.4 copy.35
  132.2 1.6 broadcast_in_dim.33
  133.7 2.3 broadcast_in_dim.32
  136.1 6.6 %while.31 = (s32[]{:T(128)}, f32[4,128,8,256]{3,2,1,0:T(8,128)}, bf16[32,128,256]{2,0,1:T(8,128)(2,1)}, s32[]{:T(128)}, s32[32]{0:T(128)S(1)}, /*index=5*/s32[]{...) while((s32[]{:T(128)}, f32[4,128,8,256]{3,2,1,0:T(8,128)}, ...), condition=%wide.region_2.3_spmd, body=%wide.region_1.2_spmd.sunk | while | flops 68159936 | bytes 48236912 | solution.py:89
  136.1 0.7 add_compare_fusion.4
  136.7 1.3 copy.62
  138.1 1.6 copy-done.1
  139.7 1.1 bitcast_add_fusion.2
  140.7 1.9 copy-done.2
  142.7 2.4 convert_element_type.73
  145.1 0.7 copy.42
  145.8 1.3 copy-done.5
  147.1 2.1 fusion.37
  149.2 0.0 reduce-scatter.3.cloned.1.call-start
  149.2 0.7 convolution_convert_fusion
  150.0 0.7 copy.43
  150.7 0.3 copy.36
  151.0 1.3 copy-done.7
  152.3 0.7 fusion.23
  152.9 0.9 copy-done.6
  153.9 1.5 fusion.36
  155.4 0.0 reduce-scatter.5.cloned.1.call-start
  155.5 4.3 broadcast_in_dim.46
  159.7 22.3 %while.32 = (s32[]{:T(128)}, f32[500,8]{1,0:T(8,128)S(1)}, f32[64,128,256]{2,1,0:T(8,128)}, s32[]{:T(128)}, s32[32]{0:T(128)S(1)}, /*index=5*/s32[32]{0:T(128)S(...) while((s32[]{:T(128)}, f32[500,8]{1,0:T(8,128)S(1)}, ...), condition=%wide.region_8.9_spmd, body=%wide.region_4.8_spmd.sunk | while | flops 337646112 | bytes 36713844 | solution.py:123
  159.7 0.7 add_compare_fusion.5
  160.4 0.1 copy.50
  160.5 0.8 scatter_fusion
  161.4 0.7 bitcast_convert_fusion.2
  162.1 0.5 copy-done.4
  162.6 3.6 convolution_bitcast_fusion.2
  166.3 5.6 %copy.51 = f32[32,128,256]{2,1,0:T(8,128)} copy(f32[32,128,256]{1,2,0:T(8,128)} %convolution_bitcast_fusion.2) | data formatting | bytes 8388608 | tf_op jit(solution)/shard_map/while/body/kij,kih->kjh/dot_general | solution.py:117
  171.9 10.2 %scatter_fusion.1 = f32[64,128,256]{2,1,0:T(8,128)} fusion(f32[64,128,256]{2,1,0:T(8,128)} %get-tuple-element.645, s32[32]{0:T(128)S(1)} %fusion.66, f32[32,128,256]{2,1,0:T(8,128)} %copy.51), kind=kCustom, calls=%fused_computation.2.clone.1 | custom fusion | flops 1048576 | bytes 12583040 | tf_op jit(solution)/shard_map/while/body/scatter-add | solution.py:118
  182.1 0.1 copy.37
  182.2 74.4 %psum.15 = f32[500,8]{0,1:T(8,128)S(1)} all-reduce(f32[500,8]{0,1:T(8,128)S(1)} %copy.37), channel_id=1, replica_groups=mesh['row'=64,'col'=4] {'row','col'}, use_global_device_ids=true, to_apply=%region_11.12 | all-reduce | flops 4000 | bytes 32000 | tf_op jit(solution)/shard_map/psum | solution.py:126
  256.6 0.6 broadcast_multiply_fusion.1
  257.2 154.0 %all-reduce.2.cloned.1.call-done = f32[2048,256]{1,0:T(8,128)} async-done(((f32[2048,256]{1,0:T(8,128)}), f32[2048,256]{1,0:T(8,128)}) %all-reduce.2.cloned.1.call-update) | async-done | bytes 2097168 | tf_op jit(solution)/shard_map/psum | solution.py:126
  411.3 3.1 broadcast_multiply_fusion
  414.4 1.5 convert_element_type.74
  415.9 2.0 fusion.27
  (36 shorter events, 0.2 us)
Async XLA Ops:
  8.0 141.2 %copy-start = (bf16[8,256,256]{2,1,0:T(8,128)(2,1)S(1)}, bf16[8,256,256]{2,1,0:T(8,128)(2,1)}, u32[]{:S(2)}) copy-start(bf16[8,256,256]{2,1,0:T(8,128)(2,1)} %param.22) | copy-start | bytes 3145732
  12.6 13.3 %copy-start.8 = (bf16[128,256]{1,0:T(8,128)(2,1)S(1)}, bf16[128,256]{1,0:T(8,128)(2,1)}, u32[]{:S(2)}) copy-start(bf16[128,256]{1,0:T(8,128)(2,1)} %param.23) | copy-start | bytes 196612
  12.6 25.6 %copy-start.13 = (s32[32]{0:T(128)S(1)}, s32[32]{0:T(128)}, u32[]{:S(2)}) copy-start(s32[32]{0:T(128)} %param.18) | copy-start | bytes 388
  12.6 25.6 %copy-start.10 = (s32[32]{0:T(128)S(1)}, s32[32]{0:T(128)}, u32[]{:S(2)}) copy-start(s32[32]{0:T(128)} %param.19) | copy-start | bytes 388
  12.6 25.6 %copy-start.11 = (bf16[500,8]{0,1:T(8,128)(2,1)S(1)}, bf16[500,8]{0,1:T(8,128)(2,1)}, u32[]{:S(2)}) copy-start(bf16[500,8]{0,1:T(8,128)(2,1)} %param.21) | copy-start | bytes 24004
  12.6 108.2 %all-to-all-start = ((bf16[64,128,256]{2,1,0:T(8,128)(2,1)}), bf16[64,128,256]{2,1,0:T(8,128)(2,1)}, u32[]{:S(2)}, u32[]{:S(2)}) async-start(bf16[64,128,256]{2,1,0:T(8,128)(2,1)} %stack.2), calls=%async_computation | async-start | bytes 8388608 | tf_op jit(solution)/shard_map/all_to_all | solution.py:12
  25.1 386.2 %all-reduce.2.cloned.1.call-start = ((), (), s32[]{:S(2)}) async-start(), calls=%async_computation.5 | async-start | bytes 4194304 | tf_op jit(solution)/shard_map/psum | solution.py:126
  38.4 86.6 %copy-start.3 = (bf16[32,128,128]{2,1,0:T(8,128)(2,1)S(1)}, bf16[32,128,128]{2,1,0:T(8,128)(2,1)}, u32[]{:S(2)}) copy-start(bf16[32,128,128]{2,1,0:T(8,128)(2,1)} %param.16) | copy-start | bytes 3145732
  133.7 2.3 copy-start.9
  136.7 2.9 copy-start.1
  140.7 1.9 copy-start.2
  145.8 1.3 copy-start.5
  149.2 265.2 %reduce-scatter.3.cloned.1.call-start = ((), (), s32[]{:S(2)}) async-start(), calls=%async_computation.3 | async-start | bytes 655360 | tf_op jit(solution)/shard_map/reduce_scatter | solution.py:92
  150.7 1.6 copy-start.7
  152.3 1.6 copy-start.6
  155.4 260.5 %reduce-scatter.5.cloned.1.call-start = ((), (), s32[]{:S(2)}) async-start(), calls=%async_computation.4 | async-start | bytes 8519680 | tf_op jit(solution)/shard_map/reduce_scatter | solution.py:125
  161.4 1.2 copy-start.4
  257.2 158.7 %copy-start.12 = (s32[256]{0:T(256)S(1)}, s32[256]{0:T(256)}, u32[]{:S(2)}) copy-start(s32[256]{0:T(256)} %param.15) | copy-start | bytes 3076
Sparse Core Ops, SparseCore 0:
  149.3 261.9 all-reduce.1
Sparse Core Ops, SparseCore 1:
  155.5 18.7 reduce-scatter.2
  182.2 149.3 reduce-scatter.4
